TPU v7x, 256 devices: a whole 4x4x8 slice. The times are simulated.
256 devices in a mesh: dp: 32 (over y_lo, z, core), tp: 8 (over x, y_hi).
Axes of the slice: x: 4, y: 4 (y_hi: 2, y_lo: 2; y = y_hi * 2 + y_lo), z: 8, core: 2. Of those that a mesh axis runs over, the one named last changes fastest.
Arguments:
- inputs: bfloat16 [1024, 8192], P(('dp', 'tp')), may hold values from -6 to 6
- out_grad: bfloat16 [1024, 8192], P(('dp', 'tp')), may hold values from -6 to 6
- gate_weight: bfloat16 [8192, 15360], P('dp', 'tp'), may hold values from -0.0625 to 0.0625
- up_weight: bfloat16 [8192, 15360], P('dp', 'tp'), may hold values from -0.0625 to 0.0625
- down_weight: bfloat16 [15360, 8192], P('tp', 'dp'), may hold values from -0.046875 to 0.046875
Outputs:
- grad_inputs: float32 [1024, 8192], P(('dp', 'tp'))
- grad_gate: float32 [8192, 15360], P('dp', 'tp')
- grad_up: float32 [8192, 15360], P('dp', 'tp')
- grad_down: float32 [15360, 8192], P('tp', 'dp')
All inputs are finite; a program needn't handle non-finite values.
Results may differ from a plain program's by a relative error of at most 0.0029.
Values may be sent and summed in bfloat16 or wider, within the bound.
A program may use at most 128 MiB of HBM per device.

v0:
```python
import jax
import jax.numpy as jnp
from jax import lax
from jax.sharding import PartitionSpec as P


def swiglu_back(gate, up_proj, back_hidden):
    sigmoid_gate = jax.nn.sigmoid(gate)
    activated = gate * sigmoid_gate
    hidden = (activated * up_proj).astype(jnp.bfloat16)
    grad_up_act = (back_hidden * activated).astype(jnp.bfloat16)
    grad_gate_act = (
        back_hidden * up_proj * sigmoid_gate * (1.0 + gate * (1.0 - sigmoid_gate))
    ).astype(jnp.bfloat16)
    return (hidden, grad_gate_act, grad_up_act)


def over_rows(left, right):
    return lax.dot_general(
        left, right, (((0,), (0,)), ((), ())), preferred_element_type=jnp.float32
    )


def over_cols(left, right):
    return lax.dot_general(
        left, right, (((1,), (1,)), ((), ())), preferred_element_type=jnp.float32
    )


def per_device(inputs, out_grad, gate_weight, up_weight, down_weight):
    input_cols, grad_cols = (
        lax.all_to_all(inputs, "dp", split_axis=1, concat_axis=0, tiled=True),
        lax.all_to_all(out_grad, "dp", split_axis=1, concat_axis=0, tiled=True),
    )
    input_all, grad_all = (
        lax.all_gather(input_cols, "tp", axis=0, tiled=True),
        lax.all_gather(grad_cols, "tp", axis=0, tiled=True),
    )
    gate_part = jnp.dot(input_all, gate_weight, preferred_element_type=jnp.float32)
    up_part = jnp.dot(input_all, up_weight, preferred_element_type=jnp.float32)
    back_part = over_cols(grad_all, down_weight)
    gate, up_proj, back_hidden = (
        lax.psum_scatter(gate_part, "dp", scatter_dimension=0, tiled=True),
        lax.psum_scatter(up_part, "dp", scatter_dimension=0, tiled=True),
        lax.psum_scatter(back_part, "dp", scatter_dimension=0, tiled=True),
    )
    hidden, grad_gate_act, grad_up_act = swiglu_back(gate, up_proj, back_hidden)
    hidden_piece = lax.all_gather(hidden, "dp", axis=0, tiled=True)
    gate_piece = lax.all_gather(grad_gate_act, "dp", axis=0, tiled=True)
    up_piece = lax.all_gather(grad_up_act, "dp", axis=0, tiled=True)
    new_gate = over_rows(input_all, gate_piece)
    new_up = over_rows(input_all, up_piece)
    new_down = over_rows(hidden_piece, grad_all)
    row_block = over_cols(gate_piece, gate_weight) + over_cols(up_piece, up_weight)
    summed = lax.psum_scatter(row_block, "tp", scatter_dimension=0, tiled=True)
    grad_inputs = lax.all_to_all(summed, "dp", split_axis=0, concat_axis=1, tiled=True)
    return (grad_inputs, new_gate, new_up, new_down)


def solution(mesh):
    in_specs = (
        P(("dp", "tp"), None),
        P(("dp", "tp"), None),
        P("dp", "tp"),
        P("dp", "tp"),
        P("tp", "dp"),
    )
    out_specs = (P(("dp", "tp"), None), P("dp", "tp"), P("dp", "tp"), P("tp", "dp"))
    return jax.shard_map(
        per_device, mesh=mesh, in_specs=in_specs, out_specs=out_specs, check_vma=False
    )
```

profile of v0, /device:TPU:16, one launch (start us, length us, event | category | flops | bytes accessed | tf_op | source)
XLA Modules:
  0.0 742.4 jit_solution(10308651327263543812)
XLA Ops:
  7.2 18.8 %all_to_all.57 = bf16[4,32,256]{2,0,1:T(4,128)(2,1)S(1)} all-to-all(bf16[4,32,256]{2,0,1:T(4,128)(2,1)} %bitcast.30), channel_id=1, replica_groups=mesh['dp'=32,'tp'=8] {'dp'}, dimensions={1} | all-to-all | bytes 131072 | tf_op jit(solution)/shard_map/all_to_all | solution.py:32
  26.0 35.1 %all_gather.16 = bf16[1024,256]{1,0:T(8,128)(2,1)S(1)} all-gather(bf16[128,256]{1,0:T(8,128)(2,1)S(1)} %all_to_all.49), channel_id=1, replica_groups=mesh['dp'=32,'tp'=8] {'tp'}, dimensions={0}, use_global_device_ids=true | all-gather | bytes 589824 | tf_op jit(solution)/shard_map/all_gather | solution.py:36
  61.1 5.5 fusion.2
  66.7 0.0 reduce-scatter.9.cloned.1.call-start
  66.7 4.4 fusion.3
  71.2 0.0 reduce-scatter.5.cloned.1.call-start
  71.2 0.8 copy-done.3
  72.0 12.3 %all_to_all.58 = bf16[4,32,256]{2,0,1:T(4,128)(2,1)S(1)} all-to-all(bf16[4,32,256]{2,0,1:T(4,128)(2,1)S(1)} %bitcast.31), channel_id=1, replica_groups=mesh['dp'=32,'tp'=8] {'dp'}, dimensions={1} | all-to-all | bytes 131072 | tf_op jit(solution)/shard_map/all_to_all | solution.py:33
  84.3 36.0 %all_gather.15 = bf16[1024,256]{1,0:T(8,128)(2,1)S(1)} all-gather(bf16[128,256]{1,0:T(8,128)(2,1)S(1)} %all_to_all.45), channel_id=1, replica_groups=mesh['dp'=32,'tp'=8] {'tp'}, dimensions={0}, use_global_device_ids=true | all-gather | bytes 589824 | tf_op jit(solution)/shard_map/all_gather | solution.py:37
  120.3 4.4 fusion.1
  124.7 0.0 all-gather.4.cloned.1.call-start
  124.8 67.8 %reduce-scatter.7.cloned.1.call-done = f32[32,1920]{1,0:T(8,128)} async-done(((f32[1024,1920]{1,0:T(8,128)}), f32[32,1920]{1,0:T(8,128)}) %reduce-scatter.7.cloned.1.call-update) | async-done | bytes 245776 | tf_op jit(solution)/shard_map/reduce_scatter | solution.py:44
  192.5 127.8 %reduce-scatter.9.cloned.1.call-done = f32[32,1920]{1,0:T(8,128)} async-done(((f32[1024,1920]{1,0:T(8,128)}), f32[32,1920]{1,0:T(8,128)}) %reduce-scatter.9.cloned.1.call-update) | async-done | bytes 245776 | tf_op jit(solution)/shard_map/reduce_scatter | solution.py:43
  320.3 126.7 %reduce-scatter.5.cloned.1.call-done = f32[32,1920]{1,0:T(8,128)} async-done(((f32[1024,1920]{1,0:T(8,128)}), f32[32,1920]{1,0:T(8,128)}) %reduce-scatter.5.cloned.1.call-update) | async-done | bytes 245776 | tf_op jit(solution)/shard_map/reduce_scatter | solution.py:45
  447.0 2.0 multiply_convert_fusion
  449.1 0.5 all-gather.6.cloned.1.call-update
  449.7 62.7 %all-gather.4.cloned.1.call-done = bf16[1024,1920]{1,0:T(8,128)(2,1)} async-done(((bf16[32,1920]{1,0:T(8,128)(2,1)}), bf16[1024,1920]{1,0:T(8,128)(2,1)}) %all-gather.4.cloned.1.call-update) | async-done | bytes 3932176 | tf_op jit(solution)/shard_map/all_gather | solution.py:49
  512.4 4.4 fusion.4
  516.7 64.4 %all-gather.6.cloned.1.call-done = bf16[1024,1920]{1,0:T(8,128)(2,1)} async-done(((bf16[32,1920]{1,0:T(8,128)(2,1)}), bf16[1024,1920]{1,0:T(8,128)(2,1)}) %all-gather.6.cloned.1.call-update) | async-done | bytes 3932176 | tf_op jit(solution)/shard_map/all_gather | solution.py:50
  581.1 4.7 convolution_add_fusion
  585.9 0.0 all-gather.8.cloned.1.call-start
  585.9 0.7 all-gather.8.cloned.1.call-update
  586.6 4.6 convolution_bitcast_fusion.1
  591.2 2.8 copy.15
  594.1 4.6 convolution_bitcast_fusion
  598.7 2.8 copy.16
  601.5 60.5 %reduce-scatter.11.cloned.1.call-done = f32[128,256]{1,0:T(8,128)} async-done(((f32[1024,256]{1,0:T(8,128)}), f32[128,256]{1,0:T(8,128)}) %reduce-scatter.11.cloned.1.call-update) | async-done | bytes 131088 | tf_op jit(solution)/shard_map/reduce_scatter | solution.py:55
  662.0 1.6 all_to_all.50
  663.6 8.0 %all-to-all-start.2 = ((f32[32,4,256]{2,1,0:T(4,128)}), f32[32,4,256]{2,1,0:T(4,128)S(1)}, u32[]{:S(2)}, u32[]{:S(2)}) async-start(f32[32,4,256]{2,1,0:T(4,128)} %all_to_all.50), calls=%async_computation.6 | async-start | bytes 262144 | tf_op jit(solution)/shard_map/all_to_all | solution.py:56
  671.6 58.7 %all-gather.8.cloned.1.call-done = bf16[1024,1920]{1,0:T(8,128)(2,1)} async-done(((bf16[32,1920]{1,0:T(8,128)(2,1)}), bf16[1024,1920]{1,0:T(8,128)(2,1)}) %all-gather.8.cloned.1.call-update) | async-done | bytes 3932176 | tf_op jit(solution)/shard_map/all_gather | solution.py:48
  730.3 4.6 fusion.5
  734.9 0.7 copy.18
  (18 shorter events, 0.3 us)
Async XLA Ops:
  7.2 59.6 %copy-start = (bf16[256,1920]{1,0:T(8,128)(2,1)S(1)}, bf16[256,1920]{1,0:T(8,128)(2,1)}, u32[]{:S(2)}) copy-start(bf16[256,1920]{1,0:T(8,128)(2,1)} %param.7) | copy-start | bytes 2949124
  7.2 185.4 %reduce-scatter.7.cloned.1.call-start = ((), (), s32[]{:S(2)}) async-start(), calls=%async_computation.8 | async-start | bytes 8110080 | tf_op jit(solution)/shard_map/reduce_scatter | solution.py:44
  66.7 253.6 %reduce-scatter.9.cloned.1.call-start = ((), (), s32[]{:S(2)}) async-start(), calls=%async_computation.9 | async-start | bytes 8110080 | tf_op jit(solution)/shard_map/reduce_scatter | solution.py:43
  71.1 0.8 copy-start.3
  71.1 49.1 %copy-start.1 = (bf16[1920,256]{1,0:T(8,128)(2,1)S(1)}, bf16[1920,256]{1,0:T(8,128)(2,1)}, u32[]{:S(2)}) copy-start(bf16[1920,256]{1,0:T(8,128)(2,1)} %param.9) | copy-start | bytes 2949124
  71.2 375.9 %reduce-scatter.5.cloned.1.call-start = ((), (), s32[]{:S(2)}) async-start(), calls=%async_computation.7 | async-start | bytes 8110080 | tf_op jit(solution)/shard_map/reduce_scatter | solution.py:45
  124.7 456.4 %copy-start.2 = (bf16[256,1920]{1,0:T(8,128)(2,1)S(1)}, bf16[256,1920]{1,0:T(8,128)(2,1)}, u32[]{:S(2)}) copy-start(bf16[256,1920]{1,0:T(8,128)(2,1)} %param.8) | copy-start | bytes 2949124
  124.7 387.7 %all-gather.4.cloned.1.call-start = ((), (), s32[]{:S(2)}) async-start(), calls=%async_computation.10 | async-start | bytes 4055040 | tf_op jit(solution)/shard_map/all_gather | solution.py:49
  449.1 132.1 %all-gather.6.cloned.1.call-start = ((), (), s32[]{:S(2)}) async-start(), calls=%async_computation.11 | async-start | bytes 4055040 | tf_op jit(solution)/shard_map/all_gather | solution.py:50
  449.7 212.3 %reduce-scatter.11.cloned.1.call-start = ((), (), s32[]{:S(2)}) async-start(), calls=%async_computation.12 | async-start | bytes 1179648 | tf_op jit(solution)/shard_map/reduce_scatter | solution.py:55
  585.9 144.5 %all-gather.8.cloned.1.call-start = ((), (), s32[]{:S(2)}) async-start(), calls=%async_computation.13 | async-start | bytes 4055040 | tf_op jit(solution)/shard_map/all_gather | solution.py:48
  663.6 71.3 %all-to-all-start.2 = ((f32[32,4,256]{2,1,0:T(4,128)}), f32[32,4,256]{2,1,0:T(4,128)S(1)}, u32[]{:S(2)}, u32[]{:S(2)}) async-start(f32[32,4,256]{2,1,0:T(4,128)} %all_to_all.50), calls=%async_computation.6 | async-start | bytes 262144 | tf_op jit(solution)/shard_map/all_to_all | solution.py:56
Sparse Core Ops, SparseCore 0:
  66.8 125.6 reduce-scatter.6
  195.3 124.9 reduce-scatter.8
  322.9 124.1 reduce-scatter.4
  449.5 62.8 all-gather.3
  514.8 66.2 all-gather.5
  586.0 75.9 reduce-scatter.10
  663.9 66.4 all-gather.7
where the time goes:
time: 745 us; the launch traced here: 742 us
  waiting for transfers between devices  570 us (77%)
  blocking collectives  102 us (14%)
  matrix products  37.2 us (5%)
  between operations  14.2 us (2%)
  local copies, waits for them, and re-layouts  8.73 us (1%)
  starting transfers between devices  8.32 us (1%)
    reduce_scatter x1, waiting for transfers between devices, per_device(): lax.psum_scatter(gate_part, 'dp', scatter_dimension=0, tiled=True)  128 us
    reduce_scatter x1, waiting for transfers between devices, per_device(): lax.psum_scatter(back_part, 'dp', scatter_dimension=0, tiled=True)  127 us
    reduce_scatter x1, waiting for transfers between devices, per_device(): lax.psum_scatter(up_part, 'dp', scatter_dimension=0, tiled=True)  67.8 us
    all_gather x1, waiting for transfers between devices, per_device(): up_piece = lax.all_gather(grad_up_act, 'dp', axis=0, tiled=True)  64.4 us
    all_gather x1, waiting for transfers between devices, per_device(): gate_piece = lax.all_gather(grad_gate_act, 'dp', axis=0, tiled=True)  62.7 us
    reduce_scatter x1, waiting for transfers between devices, per_device(): summed = lax.psum_scatter(row_block, 'tp', scatter_dimension=0, tiled=True)  60.5 us
    all_gather x1, waiting for transfers between devices, per_device(): hidden_piece = lax.all_gather(hidden, 'dp', axis=0, tiled=True)  58.7 us
    all_gather x1, blocking collectives, per_device(): lax.all_gather(grad_cols, 'tp', axis=0, tiled=True)  36 us
  transfers between devices with their start and end apart: 8, of which 7 were waited for; matrix products, arithmetic and copies ran while one was open for 4% of the time, Pallas kernels for 0%

commit v1 on v0

v1 whole, which is shorter than its diff:
```python
import jax
import jax.numpy as jnp
from jax import lax
from jax.experimental import pallas as pl
from jax.experimental.pallas import tpu as pltpu
from jax.sharding import PartitionSpec as P

MESH = pl.DeviceIdType.MESH
F32, BF16 = jnp.float32, jnp.bfloat16
NZ, NYZ, NTP = 8, 16, 8
OWN = 4
DC = 256
FF = 1920
CA = 896
HA = 512
HB = 512
UP, DOWN = 0, 1
TILES = ((0, 512), (512, 384), (896, 512), (1408, 512))


SCALE = 2.0**19
TINY = 2.0**-126


def coded(v):
    return (v * jnp.abs(v) * (v * v)).astype(BF16)


def decoded(y):
    y = y.astype(F32)
    r = lax.rsqrt(jnp.maximum(jnp.abs(y), TINY))
    return y * r * r * lax.rsqrt(r)


def dot(a, b):
    return jnp.dot(a, b, preferred_element_type=F32)


def dot_nt(a, b):
    return lax.dot_general(a, b, (((1,), (1,)), ((), ())), preferred_element_type=F32)


def kernel(
    x_ref, g_ref, wg_ref, wu_ref, wd_ref,
    gi_ref, og_ref, ou_ref, od_ref,
    stage, first, tokens, xs, xts, xtp, wgs, wus, wds, part,
    ya_s, ya_r, zb_s, zb_r, za_s, za_r, yb_s, yb_r, acts,
    gi, gi_r, fin_s, fin_r, odt,
    first_ss, first_rs, tok_ss, tok_rs, w_ls, w_ss, w_rs, xt_ss, xt_rs,
    ya_ss, ya_rs, zb_ss, zb_rs, za_ss, za_rs, yb_ss, yb_rs,
    aza_ss, aza_rs, azb_ss, azb_rs, aya_ss, aya_rs, ayb_ss, ayb_rs, core_ss, core_rs,
    gi_ss, gi_rs, fin_ss, fin_rs, out_ls,
):
    dp, tp = lax.axis_index("dp"), lax.axis_index("tp")
    c = lax.rem(dp, 2)
    yz = lax.div(dp, 2)
    z = lax.rem(yz, NZ)
    a = lax.div(yz, NZ)

    def at(yz_to):
        return (yz_to * 2 + c, tp)

    def at_z(step):
        return at(a * NZ + lax.rem(z + step + NZ, NZ))

    other_y = at((1 - a) * NZ + z)
    other_core = (yz * 2 + 1 - c, tp)
    z_next = (at_z(1), at_z(-1))

    def yz_off(k):
        return lax.rem(yz + k + NYZ, NYZ)

    def tp_off(k):
        return lax.rem(tp + k + NTP, NTP)

    def remote(src, dst, ss, rs, to):
        return pltpu.make_async_remote_copy(
            src_ref=src, dst_ref=dst, send_sem=ss, recv_sem=rs, device_id=to, device_id_type=MESH
        )

    def z_rows(step):
        return pl.ds(pl.multiple_of(lax.rem(z + step + NZ, NZ) * 32, 32), 32)

    barrier = pltpu.get_barrier_semaphore()
    for k in range(1, NYZ):
        pl.semaphore_signal(barrier, inc=1, device_id=at(yz_off(k)), device_id_type=MESH)
    for k in range(1, NTP):
        pl.semaphore_signal(barrier, inc=1, device_id=(dp, tp_off(k)), device_id_type=MESH)
    pl.semaphore_signal(barrier, inc=1, device_id=other_core, device_id_type=MESH)

    w_local = []
    mine = pl.ds(pl.multiple_of(c * DC, DC), DC)
    slots = (wgs.at[mine], wus.at[mine], wds.at[c])
    for i, (src, dst) in enumerate(zip((wg_ref, wu_ref, wd_ref), slots)):
        copy = pltpu.make_async_copy(src, dst, w_ls.at[i])
        copy.start()
        w_local.append(copy)

    for n, ref in enumerate((x_ref, g_ref)):
        whole = ref[...].astype(F32)
        for i in range(64):
            stage[i * 4 : i * 4 + 4, :] = whole[:, i * 128 : i * 128 + 128]
        first[n] = stage[0:256, :].astype(BF16).reshape(NYZ, 16, 128)

    pl.semaphore_wait(barrier, NYZ - 1 + NTP - 1 + 1)

    sends = []
    for k in range(1, NYZ):
        copy = remote(
            first.at[:, yz_off(k)], tokens.at[:, tp, yz], first_ss.at[k], first_rs.at[k], at(yz_off(k))
        )
        copy.start()
        sends.append(copy)
    for i, (src, dst) in enumerate(zip((wg_ref, wu_ref, wd_ref), slots)):
        copy = remote(src, dst, w_ss.at[i], w_rs.at[i], other_core)
        copy.start()
        sends.append(copy)
    tokens[:, tp, yz] = first[:, yz]
    for k in range(1, NYZ):
        piece = tokens.at[:, tp, yz_off(-k)]
        remote(piece, piece, first_ss.at[k], first_rs.at[k], at(yz_off(-k))).wait_recv()
    for n in range(2):
        for k in range(1, NTP):
            copy = remote(
                tokens.at[n, tp], tokens.at[n, tp], tok_ss.at[n, k], tok_rs.at[n, k], (dp, tp_off(k))
            )
            copy.start()
            sends.append(copy)

    def take_tokens(n):
        for k in range(1, NTP):
            piece = tokens.at[n, tp_off(-k)]
            remote(piece, piece, tok_ss.at[n, k], tok_rs.at[n, k], (dp, tp_off(-k))).wait_recv()
        stage[...] = tokens[n].reshape(NTP * NYZ * 16, 128).astype(F32)
        for d in range(4):
            for t in range(OWN):
                block = stage[pl.ds(d * 4 + t, 128, stride=16), :]
                rows, cols = slice(t * 128, t * 128 + 128), slice(d % 2 * 128, d % 2 * 128 + 128)
                xs[n, d // 2, rows, cols] = block.astype(BF16)
                xts[n, d // 2, cols, rows] = block.T.astype(BF16)
        copy = remote(xts.at[n, 1 - c], xtp.at[n], xt_ss.at[n], xt_rs.at[n], other_core)
        copy.start()
        sends.append(copy)

    def take_weight(i):
        w_local[i].wait()
        theirs = (
            wgs.at[pl.ds(pl.multiple_of((1 - c) * DC, DC), DC)],
            wus.at[pl.ds(pl.multiple_of((1 - c) * DC, DC), DC)],
            wds.at[1 - c],
        )[i]
        remote(theirs, theirs, w_ss.at[i], w_rs.at[i], other_core).wait_recv()

    def b_cols(direction, s):
        if s == 0:
            return (CA, CA + HB) if direction == UP else (CA + HB, FF)
        return (CA, FF)

    def a_cols(direction, s):
        if s == 0:
            return (0, HA) if direction == UP else (HA, CA)
        return (0, CA)

    def first_products(t):
        if t < 2:
            w = (wgs, wus)[t]
            for lo, size in TILES:
                cols = slice(lo, lo + size)
                value = dot(xs[0, 0], w[0:DC, cols]) + dot(xs[0, 1], w[DC : 2 * DC, cols])
                part[t, :, :, cols] = (value * SCALE).reshape(2, 256, size)
        else:
            for lo, size in TILES:
                cols = slice(lo, lo + size)
                value = dot_nt(xs[1, 0], wds[0, cols, :]) + dot_nt(xs[1, 1], wds[1, cols, :])
                part[t, :, :, cols] = (value * SCALE).reshape(2, 256, size)
        ya_s[t] = coded(part[t, 1 - a, :, 0:CA])
        copy = remote(ya_s.at[t], ya_r.at[t], ya_ss.at[t], ya_rs.at[t], other_y)
        copy.start()
        sends.append(copy)

    def b_message(buf, direction, s, t):
        lo, hi = b_cols(direction, s)
        return buf.at[direction, s, t, :, :, pl.ds(lo - CA, hi - lo)]

    def a_message(buf, direction, s, t):
        lo, hi = a_cols(direction, s)
        return buf.at[direction, s, t, :, pl.ds(lo, hi - lo)]

    def b_wait(direction, s, t):
        got = b_message(zb_r, direction, s, t)
        remote(got, got, zb_ss.at[direction, s, t], zb_rs.at[direction, s, t], z_next[direction]).wait_recv()

    def a_wait(direction, s, t):
        got = a_message(za_r, direction, s, t)
        remote(got, got, za_ss.at[direction, s, t], za_rs.at[direction, s, t], z_next[direction]).wait_recv()

    def b_step(s, t):
        for direction in (UP, DOWN):
            rows = z_rows(4 - s if direction == UP else s - 4)
            lo, hi = b_cols(direction, s)
            if s == 0:
                zb_s[direction, s, t, :, :, lo - CA : hi - CA] = coded(part[t, :, rows, lo:hi])
            else:
                b_wait(direction, s - 1, t)
                glo, ghi = b_cols(direction, s - 1)
                zb_s[direction, s, t, :, :, glo - CA : ghi - CA] = coded(
                    part[t, :, rows, glo:ghi]
                    + decoded(zb_r[direction, s - 1, t, :, :, glo - CA : ghi - CA])
                )
                if s == 1:
                    nlo, nhi = b_cols(1 - direction, 0)
                    zb_s[direction, s, t, :, :, nlo - CA : nhi - CA] = coded(part[t, :, rows, nlo:nhi])
            copy = remote(
                b_message(zb_s, direction, s, t), b_message(zb_r, direction, s, t),
                zb_ss.at[direction, s, t], zb_rs.at[direction, s, t], z_next[direction],
            )
            copy.start()
            sends.append(copy)

    def b_end(t):
        own = z_rows(0)
        for direction in (UP, DOWN):
            b_wait(direction, 3, t)
        total = part[t, :, own, CA:FF] + decoded(zb_r[UP, 3, t]) + decoded(zb_r[DOWN, 3, t])
        part[t, :, own, CA:FF] = total
        yb_s[t] = coded(part[t, 1 - a, own, CA:FF])
        copy = remote(yb_s.at[t], yb_r.at[t], yb_ss.at[t], yb_rs.at[t], other_y)
        copy.start()
        sends.append(copy)

    def a_start(t):
        remote(ya_r.at[t], ya_r.at[t], ya_ss.at[t], ya_rs.at[t], other_y).wait_recv()
        part[t, a, :, 0:CA] = part[t, a, :, 0:CA] + decoded(ya_r[t])
        a_step(0, t)

    def a_step(s, t):
        for direction in (UP, DOWN):
            rows = z_rows(4 - s if direction == UP else s - 4)
            lo, hi = a_cols(direction, s)
            if s == 0:
                za_s[direction, s, t, :, lo:hi] = coded(part[t, a, rows, lo:hi])
            else:
                a_wait(direction, s - 1, t)
                glo, ghi = a_cols(direction, s - 1)
                za_s[direction, s, t, :, glo:ghi] = coded(
                    part[t, a, rows, glo:ghi] + decoded(za_r[direction, s - 1, t, :, glo:ghi])
                )
                if s == 1:
                    nlo, nhi = a_cols(1 - direction, 0)
                    za_s[direction, s, t, :, nlo:nhi] = coded(part[t, a, rows, nlo:nhi])
            copy = remote(
                a_message(za_s, direction, s, t), a_message(za_r, direction, s, t),
                za_ss.at[direction, s, t], za_rs.at[direction, s, t], z_next[direction],
            )
            copy.start()
            sends.append(copy)

    take_tokens(0)
    take_weight(0)
    first_products(0)
    b_step(0, 0)
    take_weight(1)
    first_products(1)
    b_step(0, 1)
    take_tokens(1)
    take_weight(2)
    first_products(2)
    b_step(0, 2)
    for t in range(3):
        b_step(1, t)
    a_start(0)
    for t in range(3):
        b_step(2, t)
    a_start(1)
    a_step(1, 0)
    for t in range(3):
        b_step(3, t)
    a_start(2)
    a_step(1, 1)
    a_step(2, 0)
    for t in range(3):
        b_end(t)
    a_step(1, 2)
    a_step(2, 1)
    a_step(3, 0)
    a_step(2, 2)
    a_step(3, 1)
    a_step(3, 2)

    own = z_rows(0)
    for t in range(3):
        for direction in (UP, DOWN):
            a_wait(direction, 3, t)
        remote(yb_r.at[t], yb_r.at[t], yb_ss.at[t], yb_rs.at[t], other_y).wait_recv()

    def total(t, lo, hi):
        if hi <= CA:
            value = (
                part[t, a, own, lo:hi]
                + decoded(za_r[UP, 3, t, :, lo:hi])
                + decoded(za_r[DOWN, 3, t, :, lo:hi])
            )
        else:
            value = part[t, a, own, lo:hi] + decoded(yb_r[t, :, lo - CA : hi - CA])
        return value * (1.0 / SCALE)

    for lo, size in TILES:
        hi = lo + size
        gate, up, back = total(0, lo, hi), total(1, lo, hi), total(2, lo, hi)
        s = jax.nn.sigmoid(gate)
        silu = gate * s
        acts[0, c, a, own, lo:hi] = (back * up * s * (1.0 + gate * (1.0 - s))).astype(BF16)
        acts[1, c, a, own, lo:hi] = (back * silu).astype(BF16)
        acts[2, c, a, own, lo:hi] = (silu * up).astype(BF16)

    def hand_on(region, ss, rs, to):
        copy = remote(region, region, ss, rs, to)
        copy.start()
        return copy

    def piece_a(t, side, step, lo=0, hi=CA):
        return acts.at[t, c, side, z_rows(step), pl.ds(lo, hi - lo)]

    def piece_b(t, step, lo=CA, hi=FF):
        return acts.at[t, c, :, z_rows(step), pl.ds(lo, hi - lo)]

    def a_part(direction, s):
        return (0, CA) if s < 3 else ((0, HA) if direction == UP else (HA, CA))

    def b_part(direction, s):
        return (CA, FF) if s < 3 else ((CA, CA + HB) if direction == UP else (CA + HB, FF))

    for t in range(3):
        sends.append(
            hand_on(acts.at[t, c, a, own, pl.ds(CA, FF - CA)], ayb_ss.at[t], ayb_rs.at[t], other_y)
        )
        for direction in (UP, DOWN):
            sends.append(
                hand_on(piece_a(t, a, 0), aza_ss.at[direction, 0, t], aza_rs.at[direction, 0, t], z_next[direction])
            )
        hand_on(piece_a(t, a, 0), aya_ss.at[t], aya_rs.at[t], other_y)
        hand_on(acts.at[t, c, a, own], core_ss.at[t], core_rs.at[t], other_core)
    for t in range(3):
        theirs = acts.at[t, c, 1 - a, own, pl.ds(CA, FF - CA)]
        remote(theirs, theirs, ayb_ss.at[t], ayb_rs.at[t], other_y).wait_recv()
        for direction in (UP, DOWN):
            sends.append(
                hand_on(piece_b(t, 0), azb_ss.at[direction, 0, t], azb_rs.at[direction, 0, t], z_next[direction])
            )
        hand_on(theirs, core_ss.at[t], core_rs.at[t], other_core)

    def gather_a(s, t):
        for direction in (UP, DOWN):
            step = -1 - s if direction == UP else 1 + s
            got = piece_a(t, a, step, *a_part(direction, s))
            remote(
                got, got, aza_ss.at[direction, s, t], aza_rs.at[direction, s, t], z_next[direction]
            ).wait_recv()
            if s < 3:
                sends.append(
                    hand_on(
                        piece_a(t, a, step, *a_part(direction, s + 1)),
                        aza_ss.at[direction, s + 1, t], aza_rs.at[direction, s + 1, t], z_next[direction],
                    )
                )
            hand_on(got, aya_ss.at[t], aya_rs.at[t], other_y)
            hand_on(got, core_ss.at[t], core_rs.at[t], other_core)

    def gather_b(s, t):
        for direction in (UP, DOWN):
            step = -1 - s if direction == UP else 1 + s
            got = piece_b(t, step, *b_part(direction, s))
            remote(
                got, got, azb_ss.at[direction, s, t], azb_rs.at[direction, s, t], z_next[direction]
            ).wait_recv()
            if s < 3:
                sends.append(
                    hand_on(
                        piece_b(t, step, *b_part(direction, s + 1)),
                        azb_ss.at[direction, s + 1, t], azb_rs.at[direction, s + 1, t], z_next[direction],
                    )
                )
            hand_on(got, core_ss.at[t], core_rs.at[t], other_core)

    def gather_a_end(t):
        got = acts.at[t, c, 1 - a, :, pl.ds(0, CA)]
        remote(got, got, aya_ss.at[t], aya_rs.at[t], other_y).wait_recv()
        hand_on(got, core_ss.at[t], core_rs.at[t], other_core)

    for s in range(4):
        for t in range(3):
            gather_a(s, t)
        for t in range(3):
            gather_b(s, t)
    for t in range(3):
        gather_a_end(t)

    for t in range(OWN):
        side, rows = t // 2, slice(t % 2 * 128, t % 2 * 128 + 128)
        value = dot_nt(acts[0, c, side, rows, :], wgs[...]) + dot_nt(acts[1, c, side, rows, :], wus[...])
        gi[t] = value
    for k in range(1, NTP):
        theirs = pl.ds(pl.multiple_of(tp_off(k) * 16, 16), 16)
        copy = remote(gi.at[:, theirs], gi_r.at[tp], gi_ss.at[k], gi_rs.at[k], (dp, tp_off(k)))
        copy.start()
        sends.append(copy)

    for n in range(2):
        remote(xtp.at[n], xtp.at[n], xt_ss.at[n], xt_rs.at[n], other_core).wait_recv()

    outs = []

    def weight_gradient(t, n):
        got = acts.at[t, 1 - c]
        remote(got, got, core_ss.at[t], core_rs.at[t], other_core).wait_recv()
        for lo, size in TILES:
            cols = slice(lo, lo + size)
            value = dot(xts[n, c], acts[t, c, :, :, cols].reshape(512, size)) + dot(
                xtp[n], acts[t, 1 - c, :, :, cols].reshape(512, size)
            )
            if t < 2:
                part[t, 0, :, cols] = value
            else:
                odt[cols, :] = value.T
        src, dst = ((part.at[0, 0], og_ref), (part.at[1, 0], ou_ref), (odt, od_ref))[t]
        copy = pltpu.make_async_copy(src, dst, out_ls.at[t])
        copy.start()
        outs.append(copy)

    weight_gradient(0, 0)

    mine16 = pl.ds(pl.multiple_of(tp * 16, 16), 16)
    for k in range(1, NTP):
        got = gi_r.at[tp_off(-k)]
        remote(got, got, gi_ss.at[k], gi_rs.at[k], (dp, tp_off(-k))).wait_recv()
    gi_r[tp] = jnp.zeros((OWN, 16, 512), F32)
    for t in range(OWN):
        value = gi[t, mine16, :]
        for k in range(NTP):
            value += gi_r[k, t]
        for d in range(4):
            fin_s[pl.ds(d * 4 + t, NYZ, stride=16), :] = value[:, d * 128 : d * 128 + 128]
    for k in range(1, NYZ):
        theirs = pl.ds(pl.multiple_of(yz_off(k) * 16, 16), 16)
        copy = remote(fin_s.at[theirs], fin_r.at[yz], fin_ss.at[k], fin_rs.at[k], at(yz_off(k)))
        copy.start()
        sends.append(copy)
    fin_r[yz] = fin_s[pl.ds(pl.multiple_of(yz * 16, 16), 16), :]

    weight_gradient(1, 0)
    weight_gradient(2, 1)

    for k in range(1, NYZ):
        got = fin_r.at[yz_off(-k)]
        remote(got, got, fin_ss.at[k], fin_rs.at[k], at(yz_off(-k))).wait_recv()
    for j in range(NYZ):
        for d in range(4):
            gi_ref[:, j * 512 + d * 128 : j * 512 + d * 128 + 128] = fin_r[j, d * 4 : d * 4 + 4, :]

    for copy in sends:
        copy.wait_send()
    for t in range(3):
        sent = acts.at[t, c, a, :, pl.ds(0, CA)]
        remote(sent, sent, aya_ss.at[t], aya_rs.at[t], other_y).wait_send()
        sent = acts.at[t, c]
        remote(sent, sent, core_ss.at[t], core_rs.at[t], other_core).wait_send()
    for copy in outs:
        copy.wait()


def per_device(inputs, out_grad, gate_weight, up_weight, down_weight):
    vmem = pl.BlockSpec(memory_space=pltpu.VMEM)
    hbm = pl.BlockSpec(memory_space=pl.ANY)
    dma = pltpu.SemaphoreType.DMA
    return pl.pallas_call(
        kernel,
        out_shape=(
            jax.ShapeDtypeStruct((OWN, 8192), F32),
            jax.ShapeDtypeStruct((DC, FF), F32),
            jax.ShapeDtypeStruct((DC, FF), F32),
            jax.ShapeDtypeStruct((FF, DC), F32),
        ),
        in_specs=[vmem, vmem, hbm, hbm, hbm],
        out_specs=(vmem, hbm, hbm, hbm),
        scratch_shapes=[
            pltpu.VMEM((NTP * NYZ * 16, 128), F32),
            pltpu.VMEM((2, NYZ, 16, 128), BF16),
            pltpu.VMEM((2, NTP, NYZ, 16, 128), BF16),
            pltpu.VMEM((2, 2, 512, DC), BF16),
            pltpu.VMEM((2, 2, DC, 512), BF16),
            pltpu.VMEM((2, DC, 512), BF16),
            pltpu.VMEM((2 * DC, FF), BF16),
            pltpu.VMEM((2 * DC, FF), BF16),
            pltpu.VMEM((2, FF, DC), BF16),
            pltpu.VMEM((3, 2, 256, FF), F32),
            pltpu.VMEM((3, 256, CA), BF16),
            pltpu.VMEM((3, 256, CA), BF16),
            pltpu.VMEM((2, 4, 3, 2, 32, FF - CA), BF16),
            pltpu.VMEM((2, 4, 3, 2, 32, FF - CA), BF16),
            pltpu.VMEM((2, 4, 3, 32, CA), BF16),
            pltpu.VMEM((2, 4, 3, 32, CA), BF16),
            pltpu.VMEM((3, 32, FF - CA), BF16),
            pltpu.VMEM((3, 32, FF - CA), BF16),
            pltpu.VMEM((3, 2, 2, 256, FF), BF16),
            pltpu.VMEM((OWN, 128, 512), F32),
            pltpu.VMEM((NTP, OWN, 16, 512), F32),
            pltpu.VMEM((NYZ * 16, 128), F32),
            pltpu.VMEM((NYZ, 16, 128), F32),
            pltpu.VMEM((FF, DC), F32),
            dma((NYZ,)), dma((NYZ,)), dma((2, NTP)), dma((2, NTP)),
            dma((3,)), dma((3,)), dma((3,)), dma((2,)), dma((2,)),
            dma((3,)), dma((3,)), dma((2, 4, 3)), dma((2, 4, 3)),
            dma((2, 4, 3)), dma((2, 4, 3)), dma((3,)), dma((3,)),
            dma((2, 4, 3)), dma((2, 4, 3)), dma((2, 4, 3)), dma((2, 4, 3)),
            dma((3,)), dma((3,)), dma((3,)), dma((3,)), dma((3,)), dma((3,)),
            dma((NTP,)), dma((NTP,)), dma((NYZ,)), dma((NYZ,)), dma((3,)),
        ],
        compiler_params=pltpu.CompilerParams(
            collective_id=0, has_side_effects=True, vmem_limit_bytes=60 * 1024 * 1024
        ),
    )(inputs, out_grad, gate_weight, up_weight, down_weight)


def solution(mesh):
    in_specs = (
        P(("dp", "tp"), None),
        P(("dp", "tp"), None),
        P("dp", "tp"),
        P("dp", "tp"),
        P("tp", "dp"),
    )
    out_specs = (P(("dp", "tp"), None), P("dp", "tp"), P("dp", "tp"), P("tp", "dp"))
    return jax.shard_map(
        per_device, mesh=mesh, in_specs=in_specs, out_specs=out_specs, check_vma=False
    )
```

time: 745 us -> 157 us (0.21)
  waiting for transfers between devices: 570 us -> 0 us
  Pallas kernels: 0 us -> 148 us
  blocking collectives: 102 us -> 0 us
  matrix products: 37.2 us -> 0 us
  between operations: 14.2 us -> 0.64 us
  starting transfers between devices: 8.32 us -> 0 us
    reduce_scatter x4 -> x0, waiting for transfers between devices: 383 us -> none  [the longest x1 128 us: per_device(): lax.psum_scatter(gate_part, 'dp', scatter_dimension=0, tiled=True)]
    all_gather x3 -> x0, waiting for transfers between devices: 186 us -> none  [the longest x1 64.4 us: per_device(): up_piece = lax.all_gather(grad_up_act, 'dp', axis=0, tiled=True)]
    pallas_call x0 -> x1, Pallas kernels: none -> 148 us  [per_device(): pl.pallas_call(kernel, out_shape=(jax.ShapeDtypeStruct((OWN, 8192), F32),...]
    all_gather x2 -> x0, blocking collectives: 71.1 us -> none  [the longest x1 36 us: per_device(): lax.all_gather(grad_cols, 'tp', axis=0, tiled=True)]
    dot_general x8 -> x0, matrix products: 37.2 us -> none  [the longest x3 13.8 us: over_rows(): lax.dot_general(left, right, (((0,), (0,)), ((), ())), preferred_element_...]
    all_to_all x2 -> x0, blocking collectives: 31.1 us -> none  [the longest x1 18.8 us: per_device(): lax.all_to_all(inputs, 'dp', split_axis=1, concat_axis=0, tiled=True)]
    all_to_all x1 -> x0, starting transfers between devices: 8.03 us -> none  [per_device(): lax.all_to_all(summed, 'dp', split_axis=0, concat_axis=1, tiled=True)]
  transfers between devices with their start and end apart: 8 -> 0, of which waited for: 7 -> 0; matrix products, arithmetic and copies ran while one was open for 4% -> 0% of each run, Pallas kernels for 0% -> 0%
where the time goes in v1:
time: 157 us
  Pallas kernels  148 us (94%)
  local copies, waits for them, and re-layouts  8.18 us (5%)
    pallas_call x1, Pallas kernels, per_device(): pl.pallas_call(kernel, out_shape=(jax.ShapeDtypeStruct((OWN, 8192), F32),...  148 us
    unnamed x8, local copies, waits for them, and re-layouts  8.18 us

profile of v1, /device:TPU:16, one launch (start us, length us, event | category | flops | bytes accessed | tf_op | source)
XLA Modules:
  0.0 156.7 jit_solution(7994601516860627435)
XLA Ops:
  0.6 147.9 %shard_map.84 = (f32[4,8192]{1,0:T(4,128)}, f32[256,1920]{1,0:T(8,128)}, f32[256,1920]{1,0:T(8,128)}, f32[1920,256]{1,0:T(8,128)}) custom-call(bf16[4,8192]{1,0:T(4,128)(2,1)} %x_ref.1, bf16[4,8192]{1,0:T(4,128)(2,1)} %g_ref.1, bf16[256,1920]{1,0:T(8,128)(2,1)} %wg_ref.1, bf16[256,1920]{1,0:T(8,128)(2,1)} %wu_ref.1, bf16[1920,256]{1,0:T(8,128)(2,1)} %wd_ref.1), custom_call_target="tpu_custom_call" | custom-call | tf_op jit(solution)/shard_map/pallas_call | solution.py:475
  148.5 1.6 %copy.13 = f32[4,8192]{1,0:T(4,128)} copy(f32[4,8192]{1,0:T(4,128)} %get-tuple-element.8) | data formatting | bytes 262144
  150.1 0.0 copy-start.1
  150.1 3.1 %copy.14 = f32[256,1920]{1,0:T(8,128)} copy(f32[256,1920]{1,0:T(8,128)} %get-tuple-element.9) | data formatting | bytes 3932160
  153.2 0.0 copy-done.1
  153.2 0.0 copy-start
  153.2 1.3 copy.15
  154.4 1.0 copy-done
  155.4 1.3 copy.16
Async XLA Ops:
  150.1 3.1 %copy-start.1 = (f32[256,1920]{1,0:T(8,128)S(1)}, f32[256,1920]{1,0:T(8,128)}, u32[]{:S(2)}) copy-start(f32[256,1920]{1,0:T(8,128)} %get-tuple-element.10) | copy-start | bytes 5898244
  153.2 2.3 %copy-start = (f32[1920,256]{1,0:T(8,128)S(1)}, f32[1920,256]{1,0:T(8,128)}, u32[]{:S(2)}) copy-start(f32[1920,256]{1,0:T(8,128)} %get-tuple-element.11) | copy-start | bytes 5898244

commit v2 on v1

--- a/solution.py
+++ b/solution.py
@@ -32,6 +32,15 @@
     return y * r * r * lax.rsqrt(r)
 
 
+def squared(v):
+    return (v * jnp.abs(v)).astype(BF16)
+
+
+def rooted(y):
+    y = y.astype(F32)
+    return y * lax.rsqrt(jnp.maximum(jnp.abs(y), TINY))
+
+
 def dot(a, b):
     return jnp.dot(a, b, preferred_element_type=F32)
 
@@ -45,11 +54,11 @@
     gi_ref, og_ref, ou_ref, od_ref,
     stage, first, tokens, xs, xts, xtp, wgs, wus, wds, part,
     ya_s, ya_r, zb_s, zb_r, za_s, za_r, yb_s, yb_r, acts,
-    gi, gi_r, fin_s, fin_r, odt,
+    gi, gi_s, gi_r, fin_s, fin_r,
     first_ss, first_rs, tok_ss, tok_rs, w_ls, w_ss, w_rs, xt_ss, xt_rs,
     ya_ss, ya_rs, zb_ss, zb_rs, za_ss, za_rs, yb_ss, yb_rs,
     aza_ss, aza_rs, azb_ss, azb_rs, aya_ss, aya_rs, ayb_ss, ayb_rs, core_ss, core_rs,
-    gi_ss, gi_rs, fin_ss, fin_rs, out_ls,
+    gi_ss, gi_rs, fin_ss, fin_rs,
 ):
     dp, tp = lax.axis_index("dp"), lax.axis_index("tp")
     c = lax.rem(dp, 2)
@@ -119,7 +128,7 @@
     for k in range(1, NYZ):
         piece = tokens.at[:, tp, yz_off(-k)]
         remote(piece, piece, first_ss.at[k], first_rs.at[k], at(yz_off(-k))).wait_recv()
-    for n in range(2):
+    def tokens_start(n):
         for k in range(1, NTP):
             copy = remote(
                 tokens.at[n, tp], tokens.at[n, tp], tok_ss.at[n, k], tok_rs.at[n, k], (dp, tp_off(k))
@@ -127,17 +136,22 @@
             copy.start()
             sends.append(copy)
 
-    def take_tokens(n):
+    def tokens_wait(n):
         for k in range(1, NTP):
             piece = tokens.at[n, tp_off(-k)]
             remote(piece, piece, tok_ss.at[n, k], tok_rs.at[n, k], (dp, tp_off(-k))).wait_recv()
+
+    def tokens_end(n):
         stage[...] = tokens[n].reshape(NTP * NYZ * 16, 128).astype(F32)
         for d in range(4):
             for t in range(OWN):
                 block = stage[pl.ds(d * 4 + t, 128, stride=16), :]
                 rows, cols = slice(t * 128, t * 128 + 128), slice(d % 2 * 128, d % 2 * 128 + 128)
                 xs[n, d // 2, rows, cols] = block.astype(BF16)
-                xts[n, d // 2, cols, rows] = block.T.astype(BF16)
+
+    def transpose_tokens(n):
+        for h in range(2):
+            xts[n, h] = xs[n, h].astype(F32).T.astype(BF16)
         copy = remote(xts.at[n, 1 - c], xtp.at[n], xt_ss.at[n], xt_rs.at[n], other_core)
         copy.start()
         sends.append(copy)
@@ -255,17 +269,23 @@
             copy.start()
             sends.append(copy)
 
-    take_tokens(0)
+    tokens_start(0)
+    tokens_wait(0)
+    tokens_start(1)
+    tokens_end(0)
     take_weight(0)
     first_products(0)
     b_step(0, 0)
     take_weight(1)
     first_products(1)
     b_step(0, 1)
-    take_tokens(1)
+    tokens_wait(1)
+    tokens_end(1)
     take_weight(2)
     first_products(2)
     b_step(0, 2)
+    transpose_tokens(0)
+    transpose_tokens(1)
     for t in range(3):
         b_step(1, t)
     a_start(0)
@@ -330,7 +350,7 @@
     def b_part(direction, s):
         return (CA, FF) if s < 3 else ((CA, CA + HB) if direction == UP else (CA + HB, FF))
 
-    for t in range(3):
+    def gather_start(t):
         sends.append(
             hand_on(acts.at[t, c, a, own, pl.ds(CA, FF - CA)], ayb_ss.at[t], ayb_rs.at[t], other_y)
         )
@@ -340,7 +360,8 @@
             )
         hand_on(piece_a(t, a, 0), aya_ss.at[t], aya_rs.at[t], other_y)
         hand_on(acts.at[t, c, a, own], core_ss.at[t], core_rs.at[t], other_core)
-    for t in range(3):
+
+    def gather_start_b(t):
         theirs = acts.at[t, c, 1 - a, own, pl.ds(CA, FF - CA)]
         remote(theirs, theirs, ayb_ss.at[t], ayb_rs.at[t], other_y).wait_recv()
         for direction in (UP, DOWN):
@@ -387,28 +408,37 @@
         remote(got, got, aya_ss.at[t], aya_rs.at[t], other_y).wait_recv()
         hand_on(got, core_ss.at[t], core_rs.at[t], other_core)
 
-    for s in range(4):
-        for t in range(3):
-            gather_a(s, t)
-        for t in range(3):
-            gather_b(s, t)
-    for t in range(3):
-        gather_a_end(t)
-
-    for t in range(OWN):
+    def input_gradient(t):
         side, rows = t // 2, slice(t % 2 * 128, t % 2 * 128 + 128)
         value = dot_nt(acts[0, c, side, rows, :], wgs[...]) + dot_nt(acts[1, c, side, rows, :], wus[...])
         gi[t] = value
-    for k in range(1, NTP):
-        theirs = pl.ds(pl.multiple_of(tp_off(k) * 16, 16), 16)
-        copy = remote(gi.at[:, theirs], gi_r.at[tp], gi_ss.at[k], gi_rs.at[k], (dp, tp_off(k)))
-        copy.start()
-        sends.append(copy)
-
-    for n in range(2):
-        remote(xtp.at[n], xtp.at[n], xt_ss.at[n], xt_rs.at[n], other_core).wait_recv()
-
-    outs = []
+        gi_s[t] = squared(value)
+
+    def input_gradient_send():
+        for k in range(1, NTP):
+            theirs = pl.ds(pl.multiple_of(tp_off(k) * 16, 16), 16)
+            copy = remote(gi_s.at[:, theirs], gi_r.at[tp], gi_ss.at[k], gi_rs.at[k], (dp, tp_off(k)))
+            copy.start()
+            sends.append(copy)
+
+    def input_gradient_sum():
+        mine16 = pl.ds(pl.multiple_of(tp * 16, 16), 16)
+        for k in range(1, NTP):
+            got = gi_r.at[tp_off(-k)]
+            remote(got, got, gi_ss.at[k], gi_rs.at[k], (dp, tp_off(-k))).wait_recv()
+        gi_r[tp] = jnp.zeros((OWN, 16, 512), BF16)
+        for t in range(OWN):
+            value = gi[t, mine16, :]
+            for k in range(NTP):
+                value += rooted(gi_r[k, t])
+            for d in range(4):
+                fin_s[pl.ds(d * 4 + t, NYZ, stride=16), :] = value[:, d * 128 : d * 128 + 128]
+        for k in range(1, NYZ):
+            theirs = pl.ds(pl.multiple_of(yz_off(k) * 16, 16), 16)
+            copy = remote(fin_s.at[theirs], fin_r.at[yz], fin_ss.at[k], fin_rs.at[k], at(yz_off(k)))
+            copy.start()
+            sends.append(copy)
+        fin_r[yz] = fin_s[pl.ds(pl.multiple_of(yz * 16, 16), 16), :]
 
     def weight_gradient(t, n):
         got = acts.at[t, 1 - c]
@@ -419,35 +449,43 @@
                 xtp[n], acts[t, 1 - c, :, :, cols].reshape(512, size)
             )
             if t < 2:
-                part[t, 0, :, cols] = value
+                (og_ref, ou_ref)[t][:, cols] = value
             else:
-                odt[cols, :] = value.T
-        src, dst = ((part.at[0, 0], og_ref), (part.at[1, 0], ou_ref), (odt, od_ref))[t]
-        copy = pltpu.make_async_copy(src, dst, out_ls.at[t])
-        copy.start()
-        outs.append(copy)
-
+                od_ref[cols, :] = value.T
+
+    for t in range(2):
+        gather_start(t)
+    for t in range(2):
+        gather_start_b(t)
+    for s in range(4):
+        for t in range(2):
+            gather_a(s, t)
+        for t in range(2):
+            gather_b(s, t)
+        if s == 2:
+            gather_start(2)
+    gather_start_b(2)
+    for t in range(2):
+        gather_a_end(t)
+    input_gradient(0)
+    input_gradient(1)
+    gather_a(0, 2)
+    gather_b(0, 2)
+    input_gradient(2)
+    input_gradient(3)
+    input_gradient_send()
+    gather_a(1, 2)
+    gather_b(1, 2)
+    for n in range(2):
+        remote(xtp.at[n], xtp.at[n], xt_ss.at[n], xt_rs.at[n], other_core).wait_recv()
     weight_gradient(0, 0)
-
-    mine16 = pl.ds(pl.multiple_of(tp * 16, 16), 16)
-    for k in range(1, NTP):
-        got = gi_r.at[tp_off(-k)]
-        remote(got, got, gi_ss.at[k], gi_rs.at[k], (dp, tp_off(-k))).wait_recv()
-    gi_r[tp] = jnp.zeros((OWN, 16, 512), F32)
-    for t in range(OWN):
-        value = gi[t, mine16, :]
-        for k in range(NTP):
-            value += gi_r[k, t]
-        for d in range(4):
-            fin_s[pl.ds(d * 4 + t, NYZ, stride=16), :] = value[:, d * 128 : d * 128 + 128]
-    for k in range(1, NYZ):
-        theirs = pl.ds(pl.multiple_of(yz_off(k) * 16, 16), 16)
-        copy = remote(fin_s.at[theirs], fin_r.at[yz], fin_ss.at[k], fin_rs.at[k], at(yz_off(k)))
-        copy.start()
-        sends.append(copy)
-    fin_r[yz] = fin_s[pl.ds(pl.multiple_of(yz * 16, 16), 16), :]
-
+    gather_a(2, 2)
+    gather_b(2, 2)
     weight_gradient(1, 0)
+    gather_a(3, 2)
+    gather_b(3, 2)
+    gather_a_end(2)
+    input_gradient_sum()
     weight_gradient(2, 1)
 
     for k in range(1, NYZ):
@@ -464,8 +502,6 @@
         remote(sent, sent, aya_ss.at[t], aya_rs.at[t], other_y).wait_send()
         sent = acts.at[t, c]
         remote(sent, sent, core_ss.at[t], core_rs.at[t], other_core).wait_send()
-    for copy in outs:
-        copy.wait()
 
 
 def per_device(inputs, out_grad, gate_weight, up_weight, down_weight):
@@ -475,13 +511,13 @@
     return pl.pallas_call(
         kernel,
         out_shape=(
-            jax.ShapeDtypeStruct((OWN, 8192), F32),
-            jax.ShapeDtypeStruct((DC, FF), F32),
-            jax.ShapeDtypeStruct((DC, FF), F32),
-            jax.ShapeDtypeStruct((FF, DC), F32),
+            pltpu.VMEM((OWN, 8192), F32),
+            pltpu.VMEM((DC, FF), F32),
+            pltpu.VMEM((DC, FF), F32),
+            pltpu.VMEM((FF, DC), F32),
         ),
         in_specs=[vmem, vmem, hbm, hbm, hbm],
-        out_specs=(vmem, hbm, hbm, hbm),
+        out_specs=(vmem, vmem, vmem, vmem),
         scratch_shapes=[
             pltpu.VMEM((NTP * NYZ * 16, 128), F32),
             pltpu.VMEM((2, NYZ, 16, 128), BF16),
@@ -503,20 +539,20 @@
             pltpu.VMEM((3, 32, FF - CA), BF16),
             pltpu.VMEM((3, 2, 2, 256, FF), BF16),
             pltpu.VMEM((OWN, 128, 512), F32),
-            pltpu.VMEM((NTP, OWN, 16, 512), F32),
+            pltpu.VMEM((OWN, 128, 512), BF16),
+            pltpu.VMEM((NTP, OWN, 16, 512), BF16),
             pltpu.VMEM((NYZ * 16, 128), F32),
             pltpu.VMEM((NYZ, 16, 128), F32),
-            pltpu.VMEM((FF, DC), F32),
             dma((NYZ,)), dma((NYZ,)), dma((2, NTP)), dma((2, NTP)),
             dma((3,)), dma((3,)), dma((3,)), dma((2,)), dma((2,)),
             dma((3,)), dma((3,)), dma((2, 4, 3)), dma((2, 4, 3)),
             dma((2, 4, 3)), dma((2, 4, 3)), dma((3,)), dma((3,)),
             dma((2, 4, 3)), dma((2, 4, 3)), dma((2, 4, 3)), dma((2, 4, 3)),
             dma((3,)), dma((3,)), dma((3,)), dma((3,)), dma((3,)), dma((3,)),
-            dma((NTP,)), dma((NTP,)), dma((NYZ,)), dma((NYZ,)), dma((3,)),
+            dma((NTP,)), dma((NTP,)), dma((NYZ,)), dma((NYZ,)),
         ],
         compiler_params=pltpu.CompilerParams(
-            collective_id=0, has_side_effects=True, vmem_limit_bytes=60 * 1024 * 1024
+            collective_id=0, has_side_effects=True, vmem_limit_bytes=56 * 1024 * 1024
         ),
     )(inputs, out_grad, gate_weight, up_weight, down_weight)
 

time: 157 us -> 146 us (0.930)
  Pallas kernels: 148 us -> 141 us
  local copies, waits for them, and re-layouts: 8.18 us -> 4.47 us
    pallas_call x1, Pallas kernels: 148 us -> 141 us  [per_device(): pl.pallas_call(kernel, out_shape=(pltpu.VMEM((OWN, 8192), F32), pltpu.VME...]
    unnamed x8 -> x4, local copies, waits for them, and re-layouts: 8.18 us -> 4.47 us
where the time goes in v2:
time: 146 us
  Pallas kernels  141 us (97%)
  local copies, waits for them, and re-layouts  4.47 us (3%)
    pallas_call x1, Pallas kernels, per_device(): pl.pallas_call(kernel, out_shape=(pltpu.VMEM((OWN, 8192), F32), pltpu.VME...  141 us
    unnamed x4, local copies, waits for them, and re-layouts  4.47 us

profile of v2, /device:TPU:16, one launch (start us, length us, event | category | flops | bytes accessed | tf_op | source)
XLA Modules:
  0.0 146.0 jit_solution(16152614721986749102)
XLA Ops:
  0.6 140.9 %shard_map.84 = (f32[4,8192]{1,0:T(4,128)S(1)}, f32[256,1920]{1,0:T(8,128)S(1)}, f32[256,1920]{1,0:T(8,128)S(1)}, f32[1920,256]{1,0:T(8,128)S(1)}) custom-call(bf16[4,8192]{1,0:T(4,128)(2,1)} %x_ref.1, bf16[4,8192]{1,0:T(4,128)(2,1)} %g_ref.1, bf16[256,1920]{1,0:T(8,128)(2,1)} %wg_ref.1, bf16[256,1920]{1,0:T(8,128)(2,1)} %wu_ref.1, bf16[1920,256]{1,0:T(8,128)(2,1)} %wd_ref.1), custom_call_target="tpu_custom_call" | custom-call | tf_op jit(solution)/shard_map/pallas_call | solution.py:511
  141.5 0.7 copy.13
  142.2 1.3 copy.14
  143.4 1.3 copy.15
  144.7 1.3 copy.16

commit v3 on v2

--- a/solution.py
+++ b/solution.py
@@ -16,6 +16,7 @@
 HB = 512
 UP, DOWN = 0, 1
 TILES = ((0, 512), (512, 384), (896, 512), (1408, 512))
+FAR_FIRST = (4, 3, -3, 2, -2, 1, -1, 0)
 
 
 SCALE = 2.0**19
@@ -187,10 +188,21 @@
                 cols = slice(lo, lo + size)
                 value = dot_nt(xs[1, 0], wds[0, cols, :]) + dot_nt(xs[1, 1], wds[1, cols, :])
                 part[t, :, :, cols] = (value * SCALE).reshape(2, 256, size)
+
+    def y_send(t):
         ya_s[t] = coded(part[t, 1 - a, :, 0:CA])
-        copy = remote(ya_s.at[t], ya_r.at[t], ya_ss.at[t], ya_rs.at[t], other_y)
-        copy.start()
-        sends.append(copy)
+        for i, rows in enumerate(y_pieces(t)):
+            copy = remote(ya_s.at[t, rows], ya_r.at[t, rows], ya_ss.at[t, i], ya_rs.at[t, i], other_y)
+            copy.start()
+            sends.append(copy)
+
+    def y_pieces(t):
+        return [slice(0, 256)] if t < 2 else [z_rows(step) for step in FAR_FIRST]
+
+    def y_take(t, i):
+        rows = y_pieces(t)[i]
+        remote(ya_r.at[t, rows], ya_r.at[t, rows], ya_ss.at[t, i], ya_rs.at[t, i], other_y).wait_recv()
+        part[t, a, rows, 0:CA] = part[t, a, rows, 0:CA] + decoded(ya_r[t, rows, :])
 
     def b_message(buf, direction, s, t):
         lo, hi = b_cols(direction, s)
@@ -243,11 +255,13 @@
         sends.append(copy)
 
     def a_start(t):
-        remote(ya_r.at[t], ya_r.at[t], ya_ss.at[t], ya_rs.at[t], other_y).wait_recv()
-        part[t, a, :, 0:CA] = part[t, a, :, 0:CA] + decoded(ya_r[t])
+        y_take(t, 0)
         a_step(0, t)
 
     def a_step(s, t):
+        if t == 2 and s > 0:
+            y_take(t, 2 * s - 1)
+            y_take(t, 2 * s)
         for direction in (UP, DOWN):
             rows = z_rows(4 - s if direction == UP else s - 4)
             lo, hi = a_cols(direction, s)
@@ -276,30 +290,37 @@
     take_weight(0)
     first_products(0)
     b_step(0, 0)
+    y_send(0)
     take_weight(1)
     first_products(1)
     b_step(0, 1)
+    y_send(1)
+    b_step(1, 0)
+    b_step(1, 1)
     tokens_wait(1)
     tokens_end(1)
     take_weight(2)
     first_products(2)
     b_step(0, 2)
+    y_send(2)
+    b_step(2, 0)
+    b_step(2, 1)
+    b_step(1, 2)
     transpose_tokens(0)
     transpose_tokens(1)
-    for t in range(3):
-        b_step(1, t)
     a_start(0)
-    for t in range(3):
-        b_step(2, t)
+    b_step(3, 0)
+    b_step(3, 1)
+    b_step(2, 2)
     a_start(1)
     a_step(1, 0)
-    for t in range(3):
-        b_step(3, t)
+    b_end(0)
+    b_end(1)
+    b_step(3, 2)
     a_start(2)
     a_step(1, 1)
     a_step(2, 0)
-    for t in range(3):
-        b_end(t)
+    b_end(2)
     a_step(1, 2)
     a_step(2, 1)
     a_step(3, 0)
@@ -308,6 +329,7 @@
     a_step(3, 2)
 
     own = z_rows(0)
+    y_take(2, 7)
     for t in range(3):
         for direction in (UP, DOWN):
             a_wait(direction, 3, t)
@@ -341,8 +363,6 @@
     def piece_a(t, side, step, lo=0, hi=CA):
         return acts.at[t, c, side, z_rows(step), pl.ds(lo, hi - lo)]
 
-    def piece_b(t, step, lo=CA, hi=FF):
-        return acts.at[t, c, :, z_rows(step), pl.ds(lo, hi - lo)]
 
     def a_part(direction, s):
         return (0, CA) if s < 3 else ((0, HA) if direction == UP else (HA, CA))
@@ -360,14 +380,22 @@
             )
         hand_on(piece_a(t, a, 0), aya_ss.at[t], aya_rs.at[t], other_y)
         hand_on(acts.at[t, c, a, own], core_ss.at[t], core_rs.at[t], other_core)
+        for direction in (UP, DOWN):
+            b_hand_on(0, direction, 0, t, 0, CA, FF)
+
+    def b_hand_on(chain, direction, s, t, step, lo, hi):
+        sends.append(
+            hand_on(
+                piece_a(t, a if chain == 0 else 1 - a, step, lo, hi),
+                azb_ss.at[chain, direction, s, t], azb_rs.at[chain, direction, s, t], z_next[direction],
+            )
+        )
 
     def gather_start_b(t):
         theirs = acts.at[t, c, 1 - a, own, pl.ds(CA, FF - CA)]
         remote(theirs, theirs, ayb_ss.at[t], ayb_rs.at[t], other_y).wait_recv()
         for direction in (UP, DOWN):
-            sends.append(
-                hand_on(piece_b(t, 0), azb_ss.at[direction, 0, t], azb_rs.at[direction, 0, t], z_next[direction])
-            )
+            b_hand_on(1, direction, 0, t, 0, CA, FF)
         hand_on(theirs, core_ss.at[t], core_rs.at[t], other_core)
 
     def gather_a(s, t):
@@ -387,20 +415,15 @@
             hand_on(got, aya_ss.at[t], aya_rs.at[t], other_y)
             hand_on(got, core_ss.at[t], core_rs.at[t], other_core)
 
-    def gather_b(s, t):
+    def gather_b(s, t, chain):
         for direction in (UP, DOWN):
             step = -1 - s if direction == UP else 1 + s
-            got = piece_b(t, step, *b_part(direction, s))
+            got = piece_a(t, a if chain == 0 else 1 - a, step, *b_part(direction, s))
             remote(
-                got, got, azb_ss.at[direction, s, t], azb_rs.at[direction, s, t], z_next[direction]
+                got, got, azb_ss.at[chain, direction, s, t], azb_rs.at[chain, direction, s, t], z_next[direction]
             ).wait_recv()
             if s < 3:
-                sends.append(
-                    hand_on(
-                        piece_b(t, step, *b_part(direction, s + 1)),
-                        azb_ss.at[direction, s + 1, t], azb_rs.at[direction, s + 1, t], z_next[direction],
-                    )
-                )
+                b_hand_on(chain, direction, s + 1, t, step, *b_part(direction, s + 1))
             hand_on(got, core_ss.at[t], core_rs.at[t], other_core)
 
     def gather_a_end(t):
@@ -460,30 +483,36 @@
     for s in range(4):
         for t in range(2):
             gather_a(s, t)
-        for t in range(2):
-            gather_b(s, t)
+        for chain in range(2):
+            for t in range(2):
+                gather_b(s, t, chain)
+        if s == 1:
+            gather_start(2)
         if s == 2:
-            gather_start(2)
-    gather_start_b(2)
+            gather_start_b(2)
+    gather_a(0, 2)
+    gather_b(0, 2, 0)
+    gather_b(0, 2, 1)
     for t in range(2):
         gather_a_end(t)
     input_gradient(0)
     input_gradient(1)
-    gather_a(0, 2)
-    gather_b(0, 2)
+    gather_a(1, 2)
+    gather_b(1, 2, 0)
+    gather_b(1, 2, 1)
     input_gradient(2)
     input_gradient(3)
     input_gradient_send()
-    gather_a(1, 2)
-    gather_b(1, 2)
+    gather_a(2, 2)
+    gather_b(2, 2, 0)
+    gather_b(2, 2, 1)
     for n in range(2):
         remote(xtp.at[n], xtp.at[n], xt_ss.at[n], xt_rs.at[n], other_core).wait_recv()
     weight_gradient(0, 0)
-    gather_a(2, 2)
-    gather_b(2, 2)
+    gather_a(3, 2)
+    gather_b(3, 2, 0)
+    gather_b(3, 2, 1)
     weight_gradient(1, 0)
-    gather_a(3, 2)
-    gather_b(3, 2)
     gather_a_end(2)
     input_gradient_sum()
     weight_gradient(2, 1)
@@ -545,9 +574,9 @@
             pltpu.VMEM((NYZ, 16, 128), F32),
             dma((NYZ,)), dma((NYZ,)), dma((2, NTP)), dma((2, NTP)),
             dma((3,)), dma((3,)), dma((3,)), dma((2,)), dma((2,)),
-            dma((3,)), dma((3,)), dma((2, 4, 3)), dma((2, 4, 3)),
+            dma((3, 8)), dma((3, 8)), dma((2, 4, 3)), dma((2, 4, 3)),
             dma((2, 4, 3)), dma((2, 4, 3)), dma((3,)), dma((3,)),
-            dma((2, 4, 3)), dma((2, 4, 3)), dma((2, 4, 3)), dma((2, 4, 3)),
+            dma((2, 4, 3)), dma((2, 4, 3)), dma((2, 2, 4, 3)), dma((2, 2, 4, 3)),
             dma((3,)), dma((3,)), dma((3,)), dma((3,)), dma((3,)), dma((3,)),
             dma((NTP,)), dma((NTP,)), dma((NYZ,)), dma((NYZ,)),
         ],

time: 146 us -> 139 us (0.952)
  Pallas kernels: 141 us -> 133 us
    pallas_call x1, Pallas kernels: 141 us -> 133 us  [per_device(): pl.pallas_call(kernel, out_shape=(pltpu.VMEM((OWN, 8192), F32), pltpu.VME...]
where the time goes in v3:
time: 139 us; the launch traced here: 138 us
  Pallas kernels  133 us (96%)
  local copies, waits for them, and re-layouts  4.47 us (3%)
    pallas_call x1, Pallas kernels, per_device(): pl.pallas_call(kernel, out_shape=(pltpu.VMEM((OWN, 8192), F32), pltpu.VME...  133 us
    unnamed x4, local copies, waits for them, and re-layouts  4.47 us

profile of v3, /device:TPU:16, one launch (start us, length us, event | category | flops | bytes accessed | tf_op | source)
XLA Modules:
  0.0 138.4 jit_solution(5504321487369109484)
XLA Ops:
  0.6 133.3 %shard_map.84 = (f32[4,8192]{1,0:T(4,128)S(1)}, f32[256,1920]{1,0:T(8,128)S(1)}, f32[256,1920]{1,0:T(8,128)S(1)}, f32[1920,256]{1,0:T(8,128)S(1)}) custom-call(bf16[4,8192]{1,0:T(4,128)(2,1)} %x_ref.1, bf16[4,8192]{1,0:T(4,128)(2,1)} %g_ref.1, bf16[256,1920]{1,0:T(8,128)(2,1)} %wg_ref.1, bf16[256,1920]{1,0:T(8,128)(2,1)} %wu_ref.1, bf16[1920,256]{1,0:T(8,128)(2,1)} %wd_ref.1), custom_call_target="tpu_custom_call" | custom-call | tf_op jit(solution)/shard_map/pallas_call | solution.py:540
  133.9 0.7 copy.13
  134.6 1.3 copy.14
  135.8 1.3 copy.15
  137.1 1.3 copy.16

commit v4 on v3

--- a/solution.py
+++ b/solution.py
@@ -431,8 +431,8 @@
         remote(got, got, aya_ss.at[t], aya_rs.at[t], other_y).wait_recv()
         hand_on(got, core_ss.at[t], core_rs.at[t], other_core)
 
-    def input_gradient(t):
-        side, rows = t // 2, slice(t % 2 * 128, t % 2 * 128 + 128)
+    def input_gradient(side, i):
+        t, rows = side * 2 + i, slice(i * 128, i * 128 + 128)
         value = dot_nt(acts[0, c, side, rows, :], wgs[...]) + dot_nt(acts[1, c, side, rows, :], wus[...])
         gi[t] = value
         gi_s[t] = squared(value)
@@ -493,15 +493,15 @@
     gather_a(0, 2)
     gather_b(0, 2, 0)
     gather_b(0, 2, 1)
+    input_gradient(a, 0)
     for t in range(2):
         gather_a_end(t)
-    input_gradient(0)
-    input_gradient(1)
+    input_gradient(a, 1)
     gather_a(1, 2)
     gather_b(1, 2, 0)
     gather_b(1, 2, 1)
-    input_gradient(2)
-    input_gradient(3)
+    input_gradient(1 - a, 0)
+    input_gradient(1 - a, 1)
     input_gradient_send()
     gather_a(2, 2)
     gather_b(2, 2, 0)
@@ -513,8 +513,8 @@
     gather_b(3, 2, 0)
     gather_b(3, 2, 1)
     weight_gradient(1, 0)
+    input_gradient_sum()
     gather_a_end(2)
-    input_gradient_sum()
     weight_gradient(2, 1)
 
     for k in range(1, NYZ):

time: 139 us -> 139 us (level)
  no operation moved by 1% of the time
where the time goes in v4:
time: 139 us; the launch traced here: 138 us
  Pallas kernels  132 us (95%)
  local copies, waits for them, and re-layouts  4.47 us (3%)
    pallas_call x1, Pallas kernels, per_device(): pl.pallas_call(kernel, out_shape=(pltpu.VMEM((OWN, 8192), F32), pltpu.VME...  132 us
    unnamed x4, local copies, waits for them, and re-layouts  4.47 us

profile of v4, /device:TPU:16, one launch (start us, length us, event | category | flops | bytes accessed | tf_op | source)
XLA Modules:
  0.0 137.5 jit_solution(3964733626662761633)
XLA Ops:
  0.6 132.4 %shard_map.84 = (f32[4,8192]{1,0:T(4,128)S(1)}, f32[256,1920]{1,0:T(8,128)S(1)}, f32[256,1920]{1,0:T(8,128)S(1)}, f32[1920,256]{1,0:T(8,128)S(1)}) custom-call(bf16[4,8192]{1,0:T(4,128)(2,1)} %x_ref.1, bf16[4,8192]{1,0:T(4,128)(2,1)} %g_ref.1, bf16[256,1920]{1,0:T(8,128)(2,1)} %wg_ref.1, bf16[256,1920]{1,0:T(8,128)(2,1)} %wu_ref.1, bf16[1920,256]{1,0:T(8,128)(2,1)} %wd_ref.1), custom_call_target="tpu_custom_call" | custom-call | tf_op jit(solution)/shard_map/pallas_call | solution.py:540
  133.1 0.7 copy.13
  133.7 1.3 copy.14
  135.0 1.3 copy.15
  136.3 1.3 copy.16
